TPU v7x, 32 devices: a whole 2x2x4 slice. The times are simulated.
32 devices in a mesh: row: 8 (over z, x), col: 4 (over y, core).
Axes of the slice: x: 2, y: 2, z: 4, core: 2. Of those that a mesh axis runs over, the one named last changes fastest.
Arguments:
- descriptors: float32 [512, 64], P(('row', 'col')), may hold values from -6 to 6, as said below
- preference: float32 [512], P(('row', 'col')), may hold values from -4 to -0.5
- responsibility: float32 [512, 512], P('row', 'col'), may hold values from -6 to 4, as said below
- availability: float32 [512, 512], P('row', 'col'), may hold values from -2 to 0, as said below
Outputs:
- resp_out: float32 [512, 512], P('row', 'col')
- avail_out: float32 [512, 512], P('row', 'col')
Inputs may be any that keep to these rules, and one draw needn't show every extreme that they name: `descriptors`: descriptors 64 m + 1, 64 m + 2 and 64 m + 3 are exact copies of descriptor 64 m (where they exist); the others are independent. `responsibility`: mostly negative; positive entries are rare and scattered over the columns. `availability`: columns 64 m + 1, 64 m + 2 and 64 m + 3 are exact copies of column 64 m (where they exist); the other entries are independent.
All inputs are finite; a program needn't handle non-finite values.
Results may differ from a plain program's by a relative error of at most 0.0003.
Values sent between devices are 32-bit elements; how exact they have to be, the bound alone decides.
A program may use at most 64 MiB of HBM per device.

v0:
```python
import jax
import jax.numpy as jnp
from jax import lax
from jax.sharding import PartitionSpec as P

ITERS = 3
DAMP = 0.5
NEG_FILL = -1e30


def local(descriptors, preference, responsibility, availability):
    tile_rows, tile_cols = responsibility.shape
    row_start = lax.axis_index("row") * tile_rows
    col_start = lax.axis_index("col") * tile_cols
    all_desc, all_pref = (
        lax.all_gather(descriptors, ("row", "col"), axis=0, tiled=True),
        lax.all_gather(preference, ("row", "col"), axis=0, tiled=True),
    )
    row_desc = lax.dynamic_slice_in_dim(all_desc, row_start, tile_rows, 0)
    row_pref = lax.dynamic_slice_in_dim(all_pref, row_start, tile_rows, 0)
    col_desc = lax.dynamic_slice_in_dim(all_desc, col_start, tile_cols, 0)
    width = descriptors.shape[1]
    row_norm = jnp.sum(row_desc * row_desc, 1)
    col_norm = jnp.sum(col_desc * col_desc, 1)
    cross = lax.dot_general(
        row_desc,
        col_desc,
        (((1,), (1,)), ((), ())),
        precision=lax.Precision.HIGHEST,
        preferred_element_type=jnp.float32,
    )
    similarity = (2.0 * cross - row_norm[:, None] - col_norm[None, :]) / width
    row_ids = row_start + jnp.arange(tile_rows, dtype=jnp.int32)
    col_ids = col_start + jnp.arange(tile_cols, dtype=jnp.int32)
    diag_mask = row_ids[:, None] == col_ids[None, :]
    similarity = jnp.where(diag_mask, row_pref[:, None], similarity)
    resp_now = responsibility
    avail_now = availability
    for step_index in range(ITERS):
        summed = avail_now + similarity
        best = lax.pmax(jnp.max(summed, 1), "col")
        at_best = summed == best[:, None]
        hits = lax.psum(jnp.sum(at_best, 1, dtype=jnp.float32), "col")
        below = lax.pmax(jnp.max(jnp.where(at_best, NEG_FILL, summed), 1), "col")
        runner = jnp.where(hits >= 2.0, best, below)
        excluded = jnp.where(at_best, runner[:, None], best[:, None])
        resp_now = DAMP * resp_now + (1.0 - DAMP) * (similarity - excluded)
        kept = jnp.where(diag_mask, resp_now, jnp.maximum(resp_now, 0.0))
        column = lax.psum(jnp.sum(kept, 0), "row")
        fresh = column[None, :] - kept
        fresh = jnp.where(diag_mask, fresh, jnp.minimum(fresh, 0.0))
        avail_now = DAMP * avail_now + (1.0 - DAMP) * fresh
    return (resp_now, avail_now)


def solution(mesh):
    placed = (P(("row", "col"), None), P(("row", "col")), P("row", "col"), P("row", "col"))
    return jax.shard_map(
        local,
        mesh=mesh,
        in_specs=placed,
        out_specs=(P("row", "col"), P("row", "col")),
        check_vma=False,
    )
```

profile of v0, /device:TPU:0, one launch (start us, length us, event | category | flops | bytes accessed | tf_op | source)
XLA Modules:
  0.0 194.8 jit_solution(9699927089328162763)
XLA Ops:
  0.6 0.0 copy-start.4
  0.7 0.0 copy-start.3
  0.7 0.6 copy-done.4
  1.3 0.2 dynamic-update-slice
  1.5 42.0 %all-reduce = f32[512]{0:T(512)S(1)} all-reduce(f32[512]{0:T(512)S(1)} %dynamic-update-slice), channel_id=1, replica_groups=mesh['row'=8,'col'=4] {'row','col'}, use_global_device_ids=true, to_apply=%add | all-reduce | flops 512 | bytes 4096
  43.5 0.1 dynamic_slice.9
  43.5 0.0 copy-done.3
  43.5 40.9 %all_gather.7 = f32[512,64]{1,0:T(8,128)S(1)} all-gather(f32[16,64]{1,0:T(8,128)S(1)} %copy-done.3), channel_id=1, replica_groups=mesh['row'=8,'col'=4] {'row','col'}, dimensions={0}, use_global_device_ids=true | all-gather | bytes 135168 | tf_op jit(solution)/shard_map/all_gather | solution.py:16
  84.4 0.1 multiply_reduce_fusion
  84.5 0.0 copy-start.1
  84.5 0.1 multiply_reduce_fusion.1
  84.6 0.6 copy-done.1
  85.3 0.3 fusion.20
  85.6 0.0 copy-start
  85.6 6.0 %pmax.42 = f32[64]{0:T(128)S(1)} all-reduce(f32[64]{0:T(128)S(1)} %get-tuple-element.19), channel_id=1, replica_groups=mesh['row'=8,'col'=4] {'col'}, use_global_device_ids=true, to_apply=%region_3.4 | all-reduce | flops 64 | bytes 512 | tf_op jit(solution)/shard_map/pmax | solution.py:41
  91.6 0.2 convert_reduce_fusion.2
  91.8 5.7 %psum.42 = f32[64]{0:T(128)S(1)} all-reduce(f32[64]{0:T(128)S(1)} %get-tuple-element.6), channel_id=1, replica_groups=mesh['row'=8,'col'=4] {'col'}, use_global_device_ids=true, to_apply=%region_5.6 | all-reduce | flops 64 | bytes 512 | tf_op jit(solution)/shard_map/psum | solution.py:43
  97.5 6.7 %pmax.43 = f32[64]{0:T(128)S(1)} all-reduce(f32[64]{0:T(128)S(1)} %get-tuple-element.7), channel_id=1, replica_groups=mesh['row'=8,'col'=4] {'col'}, use_global_device_ids=true, to_apply=%region_7.8 | all-reduce | flops 64 | bytes 512 | tf_op jit(solution)/shard_map/pmax | solution.py:44
  104.2 0.0 copy-done
  104.2 0.1 fusion.13
  104.3 17.1 %psum.43 = f32[128]{0:T(128)S(1)} all-reduce(f32[128]{0:T(128)S(1)} %fusion.13), channel_id=1, replica_groups=mesh['row'=8,'col'=4] {'row'}, use_global_device_ids=true, to_apply=%region_9.10 | all-reduce | flops 128 | bytes 1024 | tf_op jit(solution)/shard_map/psum | solution.py:49
  121.5 0.2 fusion.15
  121.7 5.7 %pmax.44 = f32[64]{0:T(128)S(1)} all-reduce(f32[64]{0:T(128)S(1)} %get-tuple-element.16), channel_id=1, replica_groups=mesh['row'=8,'col'=4] {'col'}, use_global_device_ids=true, to_apply=%region_11.12 | all-reduce | flops 64 | bytes 512 | tf_op jit(solution)/shard_map/pmax | solution.py:41
  127.3 0.2 convert_reduce_fusion.1
  127.5 6.1 %psum.44 = f32[64]{0:T(128)S(1)} all-reduce(f32[64]{0:T(128)S(1)} %get-tuple-element.4), channel_id=1, replica_groups=mesh['row'=8,'col'=4] {'col'}, use_global_device_ids=true, to_apply=%region_13.14 | all-reduce | flops 64 | bytes 512 | tf_op jit(solution)/shard_map/psum | solution.py:43
  133.6 5.6 %pmax.45 = f32[64]{0:T(128)S(1)} all-reduce(f32[64]{0:T(128)S(1)} %get-tuple-element.5), channel_id=1, replica_groups=mesh['row'=8,'col'=4] {'col'}, use_global_device_ids=true, to_apply=%region_15.16 | all-reduce | flops 64 | bytes 512 | tf_op jit(solution)/shard_map/pmax | solution.py:44
  139.3 0.1 fusion.11
  139.4 19.1 %psum.45 = f32[128]{0:T(128)S(1)} all-reduce(f32[128]{0:T(128)S(1)} %get-tuple-element.13), channel_id=1, replica_groups=mesh['row'=8,'col'=4] {'row'}, use_global_device_ids=true, to_apply=%region_17.18 | all-reduce | flops 128 | bytes 1024 | tf_op jit(solution)/shard_map/psum | solution.py:49
  158.5 0.2 fusion.17
  158.7 5.7 %pmax.46 = f32[64]{0:T(128)S(1)} all-reduce(f32[64]{0:T(128)S(1)} %get-tuple-element.11), channel_id=1, replica_groups=mesh['row'=8,'col'=4] {'col'}, use_global_device_ids=true, to_apply=%region_19.20 | all-reduce | flops 64 | bytes 512 | tf_op jit(solution)/shard_map/pmax | solution.py:41
  164.4 0.2 convert_reduce_fusion
  164.6 6.7 %psum.46 = f32[64]{0:T(128)S(1)} all-reduce(f32[64]{0:T(128)S(1)} %get-tuple-element.2), channel_id=1, replica_groups=mesh['row'=8,'col'=4] {'col'}, use_global_device_ids=true, to_apply=%region_21.22 | all-reduce | flops 64 | bytes 512 | tf_op jit(solution)/shard_map/psum | solution.py:43
  171.2 5.6 %pmax.47 = f32[64]{0:T(128)S(1)} all-reduce(f32[64]{0:T(128)S(1)} %get-tuple-element.3), channel_id=1, replica_groups=mesh['row'=8,'col'=4] {'col'}, use_global_device_ids=true, to_apply=%region_23.24 | all-reduce | flops 64 | bytes 512 | tf_op jit(solution)/shard_map/pmax | solution.py:44
  176.9 0.1 fusion.12
  177.0 0.0 copy-start.2
  177.0 17.1 %psum.47 = f32[128]{0:T(128)S(1)} all-reduce(f32[128]{0:T(128)S(1)} %get-tuple-element.8), channel_id=1, replica_groups=mesh['row'=8,'col'=4] {'row'}, use_global_device_ids=true, to_apply=%region_25.26 | all-reduce | flops 128 | bytes 1024 | tf_op jit(solution)/shard_map/psum | solution.py:49
  194.1 0.7 fusion.9
  194.8 0.0 copy-done.2
  (6 shorter events, 0.0 us)
Async XLA Ops:
  0.6 0.7 copy-start.4
  0.7 42.9 %copy-start.3 = (f32[16,64]{1,0:T(8,128)S(1)}, f32[16,64]{1,0:T(8,128)}, u32[]{:S(2)}) copy-start(f32[16,64]{1,0:T(8,128)} %param.4) | copy-start | bytes 12292
  84.5 0.8 copy-start.1
  85.6 18.6 %copy-start = (f32[64,128]{1,0:T(8,128)S(1)}, f32[64,128]{1,0:T(8,128)}, u32[]{:S(2)}) copy-start(f32[64,128]{1,0:T(8,128)} %param.6) | copy-start | bytes 98308
  177.0 17.8 %copy-start.2 = (f32[64,128]{1,0:T(8,128)}, f32[64,128]{1,0:T(8,128)S(1)}, u32[]{:S(2)}) copy-start(f32[64,128]{1,0:T(8,128)S(1)} %get-tuple-element.9) | copy-start | bytes 98308
where the time goes:
time: 195 us
  blocking collectives  190 us (97%)
  other arithmetic  2.18 us (1%)
    psum x3, blocking collectives, local(): column = lax.psum(jnp.sum(kept, 0), 'row')  53.4 us
    unnamed x1, blocking collectives  42 us
    all_gather x1, blocking collectives, local(): lax.all_gather(descriptors, ('row', 'col'), axis=0, tiled=True)  40.9 us
    psum x3, blocking collectives, local(): hits = lax.psum(jnp.sum(at_best, 1, dtype=jnp.float32), 'col')  18.5 us
    pmax x3, blocking collectives, local(): below = lax.pmax(jnp.max(jnp.where(at_best, NEG_FILL, summed), 1), 'col')  18 us
    pmax x3, blocking collectives, local(): best = lax.pmax(jnp.max(summed, 1), 'col')  17.3 us

commit v1 on v0

--- a/solution.py
+++ b/solution.py
@@ -8,12 +8,24 @@
 NEG_FILL = -1e30
 
 
+def collect(array, axis, dim):
+    ways, here = (lax.axis_size(axis), lax.axis_index(axis))
+    grown, reach = (array, 1)
+    while reach < ways:
+        theirs = lax.ppermute(grown, axis, [(d, d ^ reach) for d in range(ways)])
+        mine_first = jnp.concatenate([grown, theirs], axis=dim)
+        theirs_first = jnp.concatenate([theirs, grown], axis=dim)
+        grown = jnp.where(here & reach == 0, mine_first, theirs_first)
+        reach = 2 * reach
+    return grown
+
+
 def local(descriptors, preference, responsibility, availability):
     tile_rows, tile_cols = responsibility.shape
     row_start = lax.axis_index("row") * tile_rows
     col_start = lax.axis_index("col") * tile_cols
     all_desc, all_pref = (
-        lax.all_gather(descriptors, ("row", "col"), axis=0, tiled=True),
+        collect(descriptors, ("row", "col"), 0),
         lax.all_gather(preference, ("row", "col"), axis=0, tiled=True),
     )
     row_desc = lax.dynamic_slice_in_dim(all_desc, row_start, tile_rows, 0)

time: 195 us -> 177 us (0.908)
  blocking collectives: 190 us -> 151 us
  waiting for transfers between devices: 0 us -> 11.4 us
  starting transfers between devices: 0 us -> 8.9 us
    all_gather x1 -> x0, blocking collectives: 40.9 us -> none  [local(): lax.all_gather(descriptors, ('row', 'col'), axis=0, tiled=True)]
    ppermute x0 -> x5, waiting for transfers between devices: none -> 11.4 us  [collect(): theirs = lax.ppermute(grown, axis, [(d, d ^ reach) for d in range(ways)])]
    ppermute x0 -> x5, starting transfers between devices: none -> 8.9 us  [collect(): theirs = lax.ppermute(grown, axis, [(d, d ^ reach) for d in range(ways)])]
    psum x3, blocking collectives: 53.4 us -> 56.8 us  [local(): column = lax.psum(jnp.sum(kept, 0), 'row')]
  transfers between devices with their start and end apart: 0 -> 5, of which waited for: 0 -> 4; matrix products, arithmetic and copies ran while one was open for 0% -> 0% of each run, Pallas kernels for 0% -> 0%
where the time goes in v1:
time: 177 us; the launch traced here: 176 us
  blocking collectives  151 us (85%)
  waiting for transfers between devices  11.4 us (6%)
  starting transfers between devices  8.9 us (5%)
  other arithmetic  2.25 us (1%)
    psum x3, blocking collectives, local(): column = lax.psum(jnp.sum(kept, 0), 'row')  56.8 us
    unnamed x1, blocking collectives  40.4 us
    pmax x3, blocking collectives, local(): below = lax.pmax(jnp.max(jnp.where(at_best, NEG_FILL, summed), 1), 'col')  19.1 us
    pmax x3, blocking collectives, local(): best = lax.pmax(jnp.max(summed, 1), 'col')  17.3 us
    psum x3, blocking collectives, local(): hits = lax.psum(jnp.sum(at_best, 1, dtype=jnp.float32), 'col')  17.3 us
    ppermute x5, waiting for transfers between devices, collect(): theirs = lax.ppermute(grown, axis, [(d, d ^ reach) for d in range(ways)])  11.4 us
    ppermute x5, starting transfers between devices, collect(): theirs = lax.ppermute(grown, axis, [(d, d ^ reach) for d in range(ways)])  8.9 us
  transfers between devices with their start and end apart: 5, of which 4 were waited for; matrix products, arithmetic and copies ran while one was open for 0% of the time, Pallas kernels for 0%

profile of v1, /device:TPU:0, one launch (start us, length us, event | category | flops | bytes accessed | tf_op | source)
XLA Modules:
  0.0 176.0 jit_solution(3989884299848467819)
XLA Ops:
  0.6 0.5 collective-permute-start
  1.1 0.0 copy-start.3
  1.1 1.0 collective-permute-done
  2.2 0.0 copy-done.3
  2.2 2.9 %collective-permute-start.1 = (f32[32,64]{1,0:T(8,128)S(1)}, f32[32,64]{1,0:T(8,128)S(1)}, u32[]{:S(2)}, u32[]{:S(2)}) collective-permute-start(f32[32,64]{1,0:T(8,128)S(1)} %maximum_select_fusion.4), channel_id=1, source_target_pairs={{0,2},{1,3},{2,0},{3,1},{4,6},{5,7},{6,4},{7,5},{8,10},{9,11},{10,... | collective-permute-start | bytes 24584 | tf_op jit(solution)/shard_map/ppermute | solution.py:15
  5.1 1.7 collective-permute-done.1
  6.8 2.0 %collective-permute-start.2 = (f32[64,64]{1,0:T(8,128)S(1)}, f32[64,64]{1,0:T(8,128)S(1)}, u32[]{:S(2)}, u32[]{:S(2)}) collective-permute-start(f32[64,64]{1,0:T(8,128)S(1)} %maximum_select_fusion.3), channel_id=1, source_target_pairs={{0,4},{1,5},{2,6},{3,7},{4,0},{5,1},{6,2},{7,3},{8,12},{9,13},{10,... | collective-permute-start | bytes 49160 | tf_op jit(solution)/shard_map/ppermute | solution.py:15
  8.8 1.9 %collective-permute-done.2 = f32[64,64]{1,0:T(8,128)S(1)} collective-permute-done((f32[64,64]{1,0:T(8,128)S(1)}, f32[64,64]{1,0:T(8,128)S(1)}, u32[]{:S(2)}, u32[]{:S(2)}) %collective-permute-start.2) | collective-permute-done | bytes 16416 | tf_op jit(solution)/shard_map/ppermute | solution.py:15
  10.8 2.1 %collective-permute-start.3 = (f32[128,64]{1,0:T(8,128)S(1)}, f32[128,64]{1,0:T(8,128)S(1)}, u32[]{:S(2)}, u32[]{:S(2)}) collective-permute-start(f32[128,64]{1,0:T(8,128)S(1)} %maximum_select_fusion.2), channel_id=1, source_target_pairs={{0,8},{1,9},{2,10},{3,11},{4,12},{5,13},{6,14},{7,15},{8,0},{9,1},... | collective-permute-start | bytes 98312 | tf_op jit(solution)/shard_map/ppermute | solution.py:15
  12.9 0.0 copy-start.4
  12.9 0.7 copy-done.4
  13.6 0.2 dynamic-update-slice
  13.8 40.4 %all-reduce = f32[512]{0:T(512)S(1)} all-reduce(f32[512]{0:T(512)S(1)} %dynamic-update-slice), channel_id=1, replica_groups=mesh['row'=8,'col'=4] {'row','col'}, use_global_device_ids=true, to_apply=%add | all-reduce | flops 512 | bytes 4096
  54.2 0.1 dynamic_slice.9
  54.3 0.0 collective-permute-done.3
  54.3 1.3 collective-permute-start.4
  55.6 6.8 %collective-permute-done.4 = f32[256,64]{1,0:T(8,128)S(1)} collective-permute-done((f32[256,64]{1,0:T(8,128)S(1)}, f32[256,64]{1,0:T(8,128)S(1)}, u32[]{:S(2)}, u32[]{:S(2)}) %collective-permute-start.4) | collective-permute-done | bytes 65568 | tf_op jit(solution)/shard_map/ppermute | solution.py:15
  62.4 0.1 multiply_reduce_fusion.1
  62.5 0.0 copy-start.1
  62.5 0.1 multiply_reduce_fusion
  62.7 0.6 copy-done.1
  63.3 0.3 fusion.20
  63.7 0.0 copy-start
  63.7 5.7 %pmax.42 = f32[64]{0:T(128)S(1)} all-reduce(f32[64]{0:T(128)S(1)} %get-tuple-element.19), channel_id=1, replica_groups=mesh['row'=8,'col'=4] {'col'}, use_global_device_ids=true, to_apply=%region_3.4 | all-reduce | flops 64 | bytes 512 | tf_op jit(solution)/shard_map/pmax | solution.py:53
  69.3 0.2 convert_reduce_fusion.2
  69.5 6.5 %pmax.43 = f32[64]{0:T(128)S(1)} all-reduce(f32[64]{0:T(128)S(1)} %get-tuple-element.7), channel_id=1, replica_groups=mesh['row'=8,'col'=4] {'col'}, use_global_device_ids=true, to_apply=%region_7.8 | all-reduce | flops 64 | bytes 512 | tf_op jit(solution)/shard_map/pmax | solution.py:56
  76.0 6.0 %psum.42 = f32[64]{0:T(128)S(1)} all-reduce(f32[64]{0:T(128)S(1)} %get-tuple-element.6), channel_id=1, replica_groups=mesh['row'=8,'col'=4] {'col'}, use_global_device_ids=true, to_apply=%region_5.6 | all-reduce | flops 64 | bytes 512 | tf_op jit(solution)/shard_map/psum | solution.py:55
  82.0 0.0 copy-done
  82.0 0.1 fusion.13
  82.1 20.5 %psum.43 = f32[128]{0:T(128)S(1)} all-reduce(f32[128]{0:T(128)S(1)} %fusion.13), channel_id=1, replica_groups=mesh['row'=8,'col'=4] {'row'}, use_global_device_ids=true, to_apply=%region_9.10 | all-reduce | flops 128 | bytes 1024 | tf_op jit(solution)/shard_map/psum | solution.py:61
  102.7 0.2 fusion.15
  102.9 5.9 %pmax.44 = f32[64]{0:T(128)S(1)} all-reduce(f32[64]{0:T(128)S(1)} %get-tuple-element.16), channel_id=1, replica_groups=mesh['row'=8,'col'=4] {'col'}, use_global_device_ids=true, to_apply=%region_11.12 | all-reduce | flops 64 | bytes 512 | tf_op jit(solution)/shard_map/pmax | solution.py:53
  108.8 0.2 convert_reduce_fusion.1
  109.0 5.8 %pmax.45 = f32[64]{0:T(128)S(1)} all-reduce(f32[64]{0:T(128)S(1)} %get-tuple-element.5), channel_id=1, replica_groups=mesh['row'=8,'col'=4] {'col'}, use_global_device_ids=true, to_apply=%region_15.16 | all-reduce | flops 64 | bytes 512 | tf_op jit(solution)/shard_map/pmax | solution.py:56
  114.7 5.6 %psum.44 = f32[64]{0:T(128)S(1)} all-reduce(f32[64]{0:T(128)S(1)} %get-tuple-element.4), channel_id=1, replica_groups=mesh['row'=8,'col'=4] {'col'}, use_global_device_ids=true, to_apply=%region_13.14 | all-reduce | flops 64 | bytes 512 | tf_op jit(solution)/shard_map/psum | solution.py:55
  120.4 0.1 fusion.11
  120.5 17.1 %psum.45 = f32[128]{0:T(128)S(1)} all-reduce(f32[128]{0:T(128)S(1)} %get-tuple-element.13), channel_id=1, replica_groups=mesh['row'=8,'col'=4] {'row'}, use_global_device_ids=true, to_apply=%region_17.18 | all-reduce | flops 128 | bytes 1024 | tf_op jit(solution)/shard_map/psum | solution.py:61
  137.6 0.2 fusion.17
  137.8 5.7 %pmax.46 = f32[64]{0:T(128)S(1)} all-reduce(f32[64]{0:T(128)S(1)} %get-tuple-element.11), channel_id=1, replica_groups=mesh['row'=8,'col'=4] {'col'}, use_global_device_ids=true, to_apply=%region_19.20 | all-reduce | flops 64 | bytes 512 | tf_op jit(solution)/shard_map/pmax | solution.py:53
  143.5 0.2 convert_reduce_fusion
  143.7 6.8 %pmax.47 = f32[64]{0:T(128)S(1)} all-reduce(f32[64]{0:T(128)S(1)} %get-tuple-element.3), channel_id=1, replica_groups=mesh['row'=8,'col'=4] {'col'}, use_global_device_ids=true, to_apply=%region_23.24 | all-reduce | flops 64 | bytes 512 | tf_op jit(solution)/shard_map/pmax | solution.py:56
  150.4 5.6 %psum.46 = f32[64]{0:T(128)S(1)} all-reduce(f32[64]{0:T(128)S(1)} %get-tuple-element.2), channel_id=1, replica_groups=mesh['row'=8,'col'=4] {'col'}, use_global_device_ids=true, to_apply=%region_21.22 | all-reduce | flops 64 | bytes 512 | tf_op jit(solution)/shard_map/psum | solution.py:55
  156.1 0.1 fusion.12
  156.2 0.0 copy-start.2
  156.2 19.1 %psum.47 = f32[128]{0:T(128)S(1)} all-reduce(f32[128]{0:T(128)S(1)} %get-tuple-element.8), channel_id=1, replica_groups=mesh['row'=8,'col'=4] {'row'}, use_global_device_ids=true, to_apply=%region_25.26 | all-reduce | flops 128 | bytes 1024 | tf_op jit(solution)/shard_map/psum | solution.py:61
  175.3 0.7 fusion.9
  176.0 0.0 copy-done.2
  (11 shorter events, 0.1 us)
Async XLA Ops:
  0.6 1.6 collective-permute-start
  1.1 1.0 copy-start.3
  2.2 4.6 %collective-permute-start.1 = (f32[32,64]{1,0:T(8,128)S(1)}, f32[32,64]{1,0:T(8,128)S(1)}, u32[]{:S(2)}, u32[]{:S(2)}) collective-permute-start(f32[32,64]{1,0:T(8,128)S(1)} %maximum_select_fusion.4), channel_id=1, source_target_pairs={{0,2},{1,3},{2,0},{3,1},{4,6},{5,7},{6,4},{7,5},{8,10},{9,11},{10,... | collective-permute-start | bytes 24584 | tf_op jit(solution)/shard_map/ppermute | solution.py:15
  6.8 3.9 %collective-permute-start.2 = (f32[64,64]{1,0:T(8,128)S(1)}, f32[64,64]{1,0:T(8,128)S(1)}, u32[]{:S(2)}, u32[]{:S(2)}) collective-permute-start(f32[64,64]{1,0:T(8,128)S(1)} %maximum_select_fusion.3), channel_id=1, source_target_pairs={{0,4},{1,5},{2,6},{3,7},{4,0},{5,1},{6,2},{7,3},{8,12},{9,13},{10,... | collective-permute-start | bytes 49160 | tf_op jit(solution)/shard_map/ppermute | solution.py:15
  10.8 43.5 %collective-permute-start.3 = (f32[128,64]{1,0:T(8,128)S(1)}, f32[128,64]{1,0:T(8,128)S(1)}, u32[]{:S(2)}, u32[]{:S(2)}) collective-permute-start(f32[128,64]{1,0:T(8,128)S(1)} %maximum_select_fusion.2), channel_id=1, source_target_pairs={{0,8},{1,9},{2,10},{3,11},{4,12},{5,13},{6,14},{7,15},{8,0},{9,1},... | collective-permute-start | bytes 98312 | tf_op jit(solution)/shard_map/ppermute | solution.py:15
  12.9 0.7 copy-start.4
  54.3 8.1 %collective-permute-start.4 = (f32[256,64]{1,0:T(8,128)S(1)}, f32[256,64]{1,0:T(8,128)S(1)}, u32[]{:S(2)}, u32[]{:S(2)}) collective-permute-start(f32[256,64]{1,0:T(8,128)S(1)} %maximum_select_fusion.1), channel_id=1, source_target_pairs={{0,16},{1,17},{2,18},{3,19},{4,20},{5,21},{6,22},{7,23},{8,24},{9,... | collective-permute-start | bytes 196616 | tf_op jit(solution)/shard_map/ppermute | solution.py:15
  62.5 0.8 copy-start.1
  63.7 18.4 %copy-start = (f32[64,128]{1,0:T(8,128)S(1)}, f32[64,128]{1,0:T(8,128)}, u32[]{:S(2)}) copy-start(f32[64,128]{1,0:T(8,128)} %param.6) | copy-start | bytes 98308
  156.2 19.9 %copy-start.2 = (f32[64,128]{1,0:T(8,128)}, f32[64,128]{1,0:T(8,128)S(1)}, u32[]{:S(2)}) copy-start(f32[64,128]{1,0:T(8,128)S(1)} %get-tuple-element.9) | copy-start | bytes 98308
